TPU v7x, 1024 devices: a whole 8x8x8 slice. The times are simulated.
1024 devices in a mesh: dom: 16 (over x, z_lo), orb: 64 (over z_hi, y, core).
Axes of the slice: x: 8, y: 8, z: 8 (z_hi: 4, z_lo: 2; z = z_hi * 2 + z_lo), core: 2. Of those that a mesh axis runs over, the one named last changes fastest.
Arguments:
- orbitals: float32 [128, 256, 768], P('dom', 'orb'), may hold values from -24 to 24
- potential: float32 [128, 768], P('dom'), may hold values from -2 to 2
Outputs:
- gram_blocks: float32 [2, 256, 256], P(None, 'orb', 'dom')
All inputs are finite; a program needn't handle non-finite values.
Results may differ from a plain program's by a relative error of at most 0.00005.
Values sent between devices are 32-bit elements; how exact they have to be, the bound alone decides.
A program may use at most 32 MiB of HBM per device.

v0:
```python
import jax
import jax.numpy as jnp
from jax import lax
from jax.sharding import PartitionSpec as P

NZ = 96
NY = 8
RADIUS = 6


coeffs = (
    -5369.0 / 1800.0,
    12.0 / 7.0,
    -15.0 / 56.0,
    10.0 / 189.0,
    -1.0 / 112.0,
    2.0 / 1925.0,
    -1.0 / 16632.0,
)
center_value = 6.5
half_value = 6.5


def with_halo(cells, sides, width):
    for axis, dim in sides:
        count = lax.axis_size(axis)
        head = lax.slice_in_dim(cells, 0, width, axis=dim)
        tail = lax.slice_in_dim(cells, cells.shape[dim] - width, cells.shape[dim], axis=dim)
        cells = jnp.concatenate(
            [
                lax.ppermute(tail, axis, [(i, (i + 1) % count) for i in range(count)]),
                cells,
                lax.ppermute(head, axis, [((i + 1) % count, i) for i in range(count)]),
            ],
            axis=dim,
        )
    return cells


def periodic_pad(cube, axis_index):
    extent = cube.shape[axis_index]
    lower = lax.slice_in_dim(cube, extent - RADIUS, extent, axis=axis_index)
    upper = lax.slice_in_dim(cube, 0, RADIUS, axis=axis_index)
    return jnp.concatenate([lower, cube, upper], axis=axis_index)


def stencil_apply(padded, potential, count):
    offset = (potential.shape[0] - count) // 2
    middle = padded[RADIUS : RADIUS + count]
    width = middle.shape[1]
    cube = middle.reshape(count, width, NY, NZ)
    y_padded = periodic_pad(cube, 2)
    z_padded = periodic_pad(cube, 3)
    lap = 3.0 * coeffs[0] * cube
    for step in range(1, 7):
        near = (
            padded[RADIUS + step : RADIUS + step + count]
            + padded[RADIUS - step : RADIUS - step + count]
        )
        near = near.reshape(count, width, NY, NZ)
        near = (
            near
            + y_padded[:, :, RADIUS - step : RADIUS - step + NY]
            + y_padded[:, :, RADIUS + step : RADIUS + step + NY]
        )
        near = (
            near
            + z_padded[:, :, :, RADIUS - step : RADIUS - step + NZ]
            + z_padded[:, :, :, RADIUS + step : RADIUS + step + NZ]
        )
        lap = lap + coeffs[step] * near
    return (-0.5 * lap).reshape(count, width, NY * NZ) + potential[
        offset : offset + count, None, :
    ] * middle


def apply_field(field, potential):
    padded = with_halo(field, (("dom", 0),), RADIUS)
    return stencil_apply(padded, potential, field.shape[0])


def on_device(orbitals, potential):
    planes = orbitals.shape[0]
    current = (apply_field(orbitals, potential) - center_value * orbitals) / half_value
    following = (
        2.0 * (apply_field(current, potential) - center_value * current) / half_value - orbitals
    )
    applied = apply_field(following, potential)
    filt_cells, appl_cells = (
        lax.all_to_all(following, "orb", split_axis=2, concat_axis=1, tiled=True),
        lax.all_to_all(applied, "orb", split_axis=2, concat_axis=1, tiled=True),
    )
    total_cells = planes * lax.axis_size("dom") * orbitals.shape[2]
    correlation = jnp.einsum(
        "xop,xqp->oq",
        filt_cells,
        filt_cells,
        precision=lax.Precision.HIGHEST,
        preferred_element_type=jnp.float32,
    )
    projected = jnp.einsum(
        "xop,xqp->oq",
        filt_cells,
        appl_cells,
        precision=lax.Precision.HIGHEST,
        preferred_element_type=jnp.float32,
    )
    partial_blocks = jnp.stack([correlation, projected]) / total_cells
    row_blocks = lax.psum_scatter(partial_blocks, "orb", scatter_dimension=1, tiled=True)
    return lax.psum_scatter(row_blocks, "dom", scatter_dimension=2, tiled=True)


def solution(mesh):
    return jax.shard_map(
        on_device,
        mesh=mesh,
        in_specs=(P("dom", "orb", None), P("dom", None)),
        out_specs=P(None, "orb", "dom"),
        check_vma=False,
    )
```

profile of v0, /device:TPU:1, one launch (start us, length us, event | category | flops | bytes accessed | tf_op | source)
XLA Modules:
  0.0 728.9 jit_solution(1340657596773508163)
XLA Ops:
  6.5 1.0 fusion.204
  7.6 5.7 collective-permute-start.1
  13.3 4.2 collective-permute-start
  17.6 0.9 copy.236
  18.5 0.1 reshape.73
  18.8 0.1 collective-permute-done
  19.1 0.1 reshape.78
  19.2 0.1 reshape.74
  19.4 0.1 reshape.75
  19.5 0.1 reshape.76
  19.6 0.1 reshape.77
  19.8 0.1 reshape.79
  19.9 0.8 fusion.92
  20.7 0.1 reshape.80
  21.0 0.1 reshape.81
  21.1 2.3 collective-permute-start.3
  23.5 5.4 collective-permute-start.2
  29.1 1.9 collective-permute-done.2
  31.1 0.1 reshape.86
  31.2 0.1 reshape.82
  31.4 0.1 reshape.83
  31.6 0.1 reshape.84
  31.7 0.1 reshape.85
  31.9 0.1 reshape.87
  32.0 0.8 fusion.50
  32.8 0.1 reshape.88
  32.9 0.1 fusion.194
  33.1 0.1 reshape.89
  33.2 1.9 collective-permute-start.5
  35.2 5.5 collective-permute-start.4
  40.7 0.7 copy.252
  41.5 2.4 reshape.104
  43.9 24.0 %all-to-all-start = ((f32[64,1,384]{2,1,0:T(1,128)}), f32[64,1,384]{2,1,0:T(1,128)S(1)}, u32[]{:S(2)}, u32[]{:S(2)}) async-start(f32[64,1,384]{2,1,0:T(1,128)} %reshape.104), calls=%async_computation | async-start | bytes 196608 | tf_op jit(solution)/shard_map/all_to_all | solution.py:90
  68.0 0.1 reshape.94
  68.1 0.1 reshape.90
  68.3 0.1 reshape.91
  68.5 0.1 reshape.92
  68.6 0.1 reshape.93
  68.7 0.1 reshape.95
  68.9 0.8 fusion.8
  69.9 0.7 copy.265
  70.6 2.4 reshape.106
  73.0 7.4 %all-to-all-done = f32[64,1,384]{2,1,0:T(1,128)S(1)} async-done(((f32[64,1,384]{2,1,0:T(1,128)}), f32[64,1,384]{2,1,0:T(1,128)S(1)}, u32[]{:S(2)}, u32[]{:S(2)}) %all-to-all-start) | async-done | bytes 98336 | tf_op jit(solution)/shard_map/all_to_all | solution.py:90
  80.5 5.3 all-to-all-start.1
  85.8 0.5 broadcast.77
  86.3 0.9 reduce
  87.2 1.9 reshape.105
  89.1 1.7 copy.271
  90.8 0.4 copy.255
  91.2 0.4 convolution_bitcast_fusion.1
  91.6 6.6 all-to-all-done.1
  98.3 0.9 reduce.1
  99.2 1.9 reshape.107
  101.0 1.7 copy.273
  102.8 1.8 convolution_bitcast_fusion
  104.6 0.8 maximum_multiply_fusion
  105.5 1.3 dynamic-slice
  107.5 550.2 %all-reduce.3.cloned.1.call-done = f32[2,256,256]{2,1,0:T(8,128)} async-done(((f32[2,256,256]{2,1,0:T(8,128)}), f32[2,256,256]{2,1,0:T(8,128)}) %all-reduce.3.cloned.1.call-update) | async-done | bytes 524304
  657.7 0.7 constant_dynamic-slice_fusion
  658.4 0.2 copy.276
  658.6 0.8 reshape.101
  659.5 61.1 %reduce-scatter.5.cloned.1.call-done = f32[16,8]{1,0:T(8,128)} async-done(((f32[256,8]{1,0:T(8,128)}), f32[16,8]{1,0:T(8,128)}) %reduce-scatter.5.cloned.1.call-update) | async-done | bytes 528
  720.6 0.8 reshape.102
  721.3 0.7 copy.277
  (52 shorter events, 1.6 us)
Async XLA Ops:
  6.5 12.2 %copy-start = (f32[8,4,768]{2,1,0:T(4,128)S(1)}, f32[8,4,768]{2,1,0:T(4,128)}, u32[]{:S(2)}) copy-start(f32[8,4,768]{2,1,0:T(4,128)} %param.2) | copy-start | bytes 294916
  6.5 12.2 %copy-start.1 = (f32[8,768]{1,0:T(8,128)S(1)}, f32[8,768]{1,0:T(8,128)}, u32[]{:S(2)}) copy-start(f32[8,768]{1,0:T(8,128)} %param.3) | copy-start | bytes 73732
  7.6 11.2 %collective-permute-start.1 = (f32[6,4,768]{2,1,0:T(4,128)S(1)}, f32[6,4,768]{2,1,0:T(4,128)S(1)}, u32[]{:S(2)}, u32[]{:S(2)}) collective-permute-start(f32[6,4,768]{2,1,0:T(4,128)S(1)} %get-tuple-element.40), channel_id=1, source_target_pairs={{0,64},{64,128},{128,192},{192,256},{256,320},{320,384},{384,448},... | collective-permute-start | bytes 221192 | tf_op jit(solution)/shard_map/ppermute | solution.py:31
  13.3 5.6 collective-permute-start
  21.1 7.9 %collective-permute-start.3 = (f32[6,4,768]{2,1,0:T(4,128)S(1)}, f32[6,4,768]{2,1,0:T(4,128)S(1)}, u32[]{:S(2)}, u32[]{:S(2)}) collective-permute-start(f32[6,4,768]{2,1,0:T(4,128)S(1)} %get-tuple-element.38), channel_id=1, source_target_pairs={{0,64},{64,128},{128,192},{192,256},{256,320},{320,384},{384,448},... | collective-permute-start | bytes 221192 | tf_op jit(solution)/shard_map/ppermute | solution.py:31
  23.5 7.5 %collective-permute-start.2 = (f32[6,4,768]{2,1,0:T(4,128)S(1)}, f32[6,4,768]{2,1,0:T(4,128)S(1)}, u32[]{:S(2)}, u32[]{:S(2)}) collective-permute-start(f32[6,4,768]{2,1,0:T(4,128)S(1)} %get-tuple-element.37), channel_id=1, source_target_pairs={{64,0},{128,64},{192,128},{256,192},{320,256},{384,320},{448,384},... | collective-permute-start | bytes 221192 | tf_op jit(solution)/shard_map/ppermute | solution.py:33
  33.2 34.6 %collective-permute-start.5 = (f32[6,4,768]{2,1,0:T(4,128)S(1)}, f32[6,4,768]{2,1,0:T(4,128)S(1)}, u32[]{:S(2)}, u32[]{:S(2)}) collective-permute-start(f32[6,4,768]{2,1,0:T(4,128)S(1)} %get-tuple-element.36), channel_id=1, source_target_pairs={{0,64},{64,128},{128,192},{192,256},{256,320},{320,384},{384,448},... | collective-permute-start | bytes 221192 | tf_op jit(solution)/shard_map/ppermute | solution.py:31
  35.2 32.7 %collective-permute-start.4 = (f32[6,4,768]{2,1,0:T(4,128)S(1)}, f32[6,4,768]{2,1,0:T(4,128)S(1)}, u32[]{:S(2)}, u32[]{:S(2)}) collective-permute-start(f32[6,4,768]{2,1,0:T(4,128)S(1)} %get-tuple-element.35), channel_id=1, source_target_pairs={{64,0},{128,64},{192,128},{256,192},{320,256},{384,320},{448,384},... | collective-permute-start | bytes 221192 | tf_op jit(solution)/shard_map/ppermute | solution.py:33
  43.9 36.6 %all-to-all-start = ((f32[64,1,384]{2,1,0:T(1,128)}), f32[64,1,384]{2,1,0:T(1,128)S(1)}, u32[]{:S(2)}, u32[]{:S(2)}) async-start(f32[64,1,384]{2,1,0:T(1,128)} %reshape.104), calls=%async_computation | async-start | bytes 196608 | tf_op jit(solution)/shard_map/all_to_all | solution.py:90
  80.5 17.8 %all-to-all-start.1 = ((f32[64,1,384]{2,1,0:T(1,128)}), f32[64,1,384]{2,1,0:T(1,128)S(1)}, u32[]{:S(2)}, u32[]{:S(2)}) async-start(f32[64,1,384]{2,1,0:T(1,128)} %reshape.106), calls=%async_computation.1 | async-start | bytes 196608 | tf_op jit(solution)/shard_map/all_to_all | solution.py:91
  85.7 572.0 %all-reduce.3.cloned.1.call-start = ((), (), s32[]{:S(2)}) async-start(), calls=%async_computation.4 | async-start | bytes 1048576
  105.5 615.1 %reduce-scatter.5.cloned.1.call-start = ((), (), s32[]{:S(2)}) async-start(), calls=%async_computation.3 | async-start | bytes 139264
Sparse Core Ops, SparseCore 0:
  105.6 552.0 all-reduce.2
  661.4 59.0 reduce-scatter.4
where the time goes:
time: 740 us; the launch traced here: 729 us
  waiting for transfers between devices  628 us (85%)
  starting transfers between devices  54.5 us (7%)
  local copies, waits for them, and re-layouts  24.2 us (3%)
  between operations  14.6 us (2%)
    unnamed x4, waiting for transfers between devices  611 us
    all_to_all x1, starting transfers between devices, on_device(): lax.all_to_all(following, 'orb', split_axis=2, concat_axis=1, tiled=True)  24 us
    ppermute x3, starting transfers between devices, with_halo(): lax.ppermute(head, axis, [((i + 1) % count, i) for i in range(count)])  15.1 us
  transfers between devices with their start and end apart: 10, of which 7 were waited for; matrix products, arithmetic and copies ran while one was open for 2% of the time, Pallas kernels for 0%

commit v1 on v0

v1 whole, which is shorter than its diff:
```python
import jax
import jax.numpy as jnp
from jax import lax
from jax.experimental import pallas as pl
from jax.experimental.pallas import tpu as pltpu
from jax.sharding import PartitionSpec as P

NZ = 96
NY = 8
CELLS = 98304
MESH = pl.DeviceIdType.MESH

coeffs = (
    -5369.0 / 1800.0,
    12.0 / 7.0,
    -15.0 / 56.0,
    10.0 / 189.0,
    -1.0 / 112.0,
    2.0 / 1925.0,
    -1.0 / 16632.0,
)
CENTER = 6.5
HALF = 6.5

LEFT = 12
EXT = 46
FIRST = 34
SECOND = 22
OWN = 16


def place(x, y, z, core):
    return {"dom": x * 2 + z % 2, "orb": (z // 2) * 16 + y * 2 + core}


def in_plane(tile, scale):
    along_z = [pltpu.roll(tile, j, 1) + pltpu.roll(tile, 128 - j, 1) for j in range(1, 7)]
    turned = [None] + [pltpu.roll(tile, k, 0) for k in range(1, 8)]
    along_y = (scale * coeffs[1]) * (turned[1] + turned[7])
    along_y += (scale * (coeffs[2] + coeffs[6])) * (turned[2] + turned[6])
    along_y += (scale * (coeffs[3] + coeffs[5])) * (turned[3] + turned[5])
    along_y += (scale * 2.0 * coeffs[4]) * turned[4]
    return along_z, along_y


def wrap_lanes(tile, lane):
    tile = jnp.where(lane >= NZ, pltpu.roll(tile, NZ, 1), tile)
    return jnp.where(lane >= 112, pltpu.roll(tile, 32, 1), tile)


def kernel(
    orb_ref,
    pot_ref,
    out_ref,
    raw,
    raw_pot,
    field0,
    field1,
    field2,
    poten,
    send_y,
    recv_y,
    recv_zc,
    rows_f,
    rows_g,
    cols_f,
    cols_g,
    part,
    part_core,
    sums_y,
    part_y,
    sums_x,
    part_x,
    sums_z,
    part_z,
    halo_out,
    halo_in,
    y_out,
    y_in,
    zc_out,
    zc_in,
    core_out,
    core_in,
    ry_out,
    ry_in,
    rx_out,
    rx_in,
    rz_out,
    rz_in,
):
    dom = lax.axis_index("dom")
    orb = lax.axis_index("orb")
    x, zl = dom // 2, dom % 2
    core, y, zh = orb % 2, (orb // 2) % 8, orb // 16
    z = zh * 2 + zl
    zc = z * 2 + core
    right, left = (x + 1) % 8, (x + 7) % 8
    right2, left2 = (x + 2) % 8, (x + 6) % 8
    pair = z + 1 - 2 * zl
    z0 = zh * 2
    lane = lax.broadcasted_iota(jnp.int32, (8, 128), 1)

    barrier = pltpu.get_barrier_semaphore()

    def greet(device):
        pl.semaphore_signal(barrier, inc=1, device_id=device, device_id_type=MESH)

    for i in range(1, 8):
        greet(place(x, y ^ i, z, core))
        greet(place(x ^ i, y, z, core))
    for i in range(1, 16):
        other = zc ^ i
        greet(place(x, y, other // 2, other % 2))
    greet(place(right, y, pair, core))
    greet(place(left, y, pair, core))

    @pl.when(zl == 1)
    def _():
        greet(place(right2, y, pair, core))

    own_row = pl.multiple_of(24 + 16 * zl, 8)
    raw[pl.ds(own_row, 16), :] = orb_ref[zl]
    own_pot = pl.multiple_of(16 + 8 * zl, 8)
    raw_pot[pl.ds(own_pot, 8), :] = pot_ref[...]
    pl.semaphore_wait(barrier, 32 - zl)

    def orb_copy(half, start, count, row, slot, device):
        return pltpu.make_async_remote_copy(
            src_ref=orb_ref.at[half, pl.ds(start, count)],
            dst_ref=raw.at[pl.ds(row, count)],
            send_sem=halo_out.at[slot],
            recv_sem=halo_in.at[slot],
            device_id=device,
            device_id_type=MESH,
        )

    def pot_copy(row, slot, device, out_slot):
        return pltpu.make_async_remote_copy(
            src_ref=pot_ref,
            dst_ref=raw_pot.at[pl.ds(row, 8)],
            send_sem=halo_out.at[out_slot],
            recv_sem=halo_in.at[slot],
            device_id=device,
            device_id_type=MESH,
        )

    copies = [(orb_copy(1 - zl, 0, 16, own_row, 0, place(x, y, pair, core)), None)]
    pots = [(pot_copy(own_pot, 6, place(x, y, pair, core), 8), None)]
    for t in range(2):
        to_left = place(left, y, z0 + t, core)
        to_right = place(right, y, z0 + t, core)
        to_left2 = place(left2, y, z0 + t, core)
        for mine in range(2):
            row = 56 + 16 * mine
            slot = 1 + mine
            copies.append((to_left, t, mine, 0, 16, row, slot))
            pots.append((to_left, mine, 32 + 8 * mine, 7 + mine))
        copies.append((to_right, t, 0, 8, 8, 0, 4))
        copies.append((to_right, t, 1, 0, 16, 8, 5))
        pots.append((to_right, 1, 8, 9))
        copies.append((to_left2, t, 0, 0, 4, 88, 3))

    copies[0][0].start()
    pots[0][0].start()

    def guarded(mine, action):
        pl.when(zl == mine)(action)

    def outgoing(mine):
        result = []
        at = 1
        for device, t, who, start, count, row, slot in copies[1:]:
            if who == mine:
                result.append(
                    pltpu.make_async_remote_copy(
                        src_ref=orb_ref.at[t, pl.ds(start, count)],
                        dst_ref=raw.at[pl.ds(row, count)],
                        send_sem=halo_out.at[at],
                        recv_sem=halo_in.at[slot],
                        device_id=device,
                        device_id_type=MESH,
                    )
                )
                at += 1
        at = 9
        for device, who, row, slot in pots[1:]:
            if who == mine:
                result.append(pot_copy(row, slot, device, at))
                at += 1
        return result

    for mine in range(2):

        @pl.when(zl == mine)
        def _(mine=mine):
            for copy in outgoing(mine):
                copy.start()

    me = place(x, y, pair, core)
    orb_copy(0, 0, 16, pl.multiple_of(40 - 16 * zl, 8), 0, me).wait_recv()
    orb_copy(0, 0, 16, 56, 1, me).wait_recv()
    orb_copy(0, 0, 16, 72, 2, me).wait_recv()
    orb_copy(0, 0, 4, 88, 3, me).wait_recv()
    orb_copy(0, 8, 8, 0, 4, me).wait_recv()
    orb_copy(0, 0, 16, 8, 5, me).wait_recv()
    pot_copy(pl.multiple_of(24 - 8 * zl, 8), 6, me, 8).wait_recv()
    for slot, row in ((7, 32), (8, 40), (9, 8)):
        pot_copy(row, slot, me, 8).wait_recv()

    def spread(block, _):
        row = pl.multiple_of(block * 8, 8)
        for yy in range(NY):
            tile = raw[pl.ds(row, 8), NZ * yy : NZ * yy + NZ]
            tile = jnp.concatenate([tile, tile[:, :16], tile[:, NZ - 16 :]], axis=1)
            field0[pl.ds(row * 8 + yy, 8, stride=8), :] = tile
        return 0

    lax.fori_loop(0, 12, spread, 0)

    def spread_pot(block, _):
        row = pl.multiple_of(block * 8, 8)
        for yy in range(NY):
            tile = raw_pot[pl.ds(row, 8), NZ * yy : NZ * yy + NZ]
            tile = jnp.concatenate([tile, tile[:, :32]], axis=1)
            poten[pl.ds(row * 8 + yy, 8, stride=8), :] = tile
        return 0

    lax.fori_loop(1, 6, spread_pot, 0)

    def load(ref, plane, k):
        return ref[pl.ds(pl.multiple_of((plane * 2 + k) * 8, 8), 8), :]

    def shifted(ref, plane, k, scale, diagonal):
        tile = load(ref, plane, k)
        along_z, total = in_plane(tile, scale)
        for j in range(1, 7):
            near = along_z[j - 1] + (load(ref, plane + j, k) + load(ref, plane - j, k))
            total += (scale * coeffs[j]) * near
        return total + diagonal * tile, tile

    def potential(plane):
        return poten[pl.ds(pl.multiple_of((plane + 16) * 8, 8), 8), :]

    def first(step, _):
        for part_of in range(2):
            at = step * 2 + part_of
            diagonal = potential(at - 6) * (1.0 / HALF) + ((-1.5 * coeffs[0] - CENTER) / HALF)
            for k in range(2):
                total, _tile = shifted(field0, at + 6, k, -0.5 / HALF, diagonal)
                row = pl.multiple_of((at * 2 + k) * 8, 8)
                field1[pl.ds(row, 8), :] = wrap_lanes(total, lane)
        return 0

    lax.fori_loop(0, FIRST // 2, first, 0)

    def second(step, _):
        for part_of in range(2):
            at = step * 2 + part_of
            diagonal = potential(at) * (2.0 / HALF) + (2.0 * (-1.5 * coeffs[0] - CENTER) / HALF)
            for k in range(2):
                total, _tile = shifted(field1, at + 6, k, -1.0 / HALF, diagonal)
                total -= load(field0, at + LEFT, k)
                row = pl.multiple_of((at * 2 + k) * 8, 8)
                field2[pl.ds(row, 8), :] = wrap_lanes(total, lane)
        return 0

    lax.fori_loop(0, SECOND // 2, second, 0)

    rows_out = send_y.reshape(512, 128)

    def third(step, _):
        for part_of in range(2):
            at = step * 2 + part_of
            diagonal = potential(at) * 0.5 - 0.75 * coeffs[0]
            for k in range(2):
                tile = load(field2, at, k)
                along_z, total = in_plane(tile, -0.25)
                for j in range(1, 7):
                    near = along_z[j - 1] + 2.0 * load(field2, at + j, k)
                    total += (-0.25 * coeffs[j]) * near
                total += diagonal * tile
                rows_out[pl.ds(at * 4 + k, 8, stride=64), :] = jnp.where(lane < NZ, tile, 0.0)
                rows_out[pl.ds(at * 4 + 2 + k, 8, stride=64), :] = jnp.where(lane < NZ, total, 0.0)
        return 0

    lax.fori_loop(0, OWN // 2, third, 0)

    def y_copy(i):
        return pltpu.make_async_remote_copy(
            src_ref=send_y.at[y ^ i],
            dst_ref=recv_y.at[y],
            send_sem=y_out.at[i],
            recv_sem=y_in.at[i],
            device_id=place(x, y ^ i, z, core),
            device_id_type=MESH,
        )

    for i in range(1, 8):
        y_copy(i).start()
    recv_y[y] = send_y[y]
    for i in range(1, 8):
        y_copy(i).wait_recv()

    def zc_copy(i):
        other = zc ^ i
        return pltpu.make_async_remote_copy(
            src_ref=recv_y.at[:, other],
            dst_ref=recv_zc.at[pl.ds(zc * 8, 8)],
            send_sem=zc_out.at[i],
            recv_sem=zc_in.at[i],
            device_id=place(x, y, other // 2, other % 2),
            device_id_type=MESH,
        )

    for i in range(1, 16):
        zc_copy(i).start()
    recv_zc[pl.ds(zc * 8, 8)] = recv_y[:, zc]
    for i in range(1, 16):
        zc_copy(i).wait_recv()

    flat = recv_zc.reshape(512, 128)
    for zz in range(8):
        for k in range(2):
            for what, rows in ((0, rows_f), (2, rows_g)):
                rows[pl.ds(zz * 2 + k, 16, stride=16), :] = flat[
                    pl.ds(zz * 64 + what + k, 16, stride=4), :
                ]
            for cc in range(2):
                at = (zz // 2) * 64 + cc * 4 + (zz % 2) * 2 + k
                for what, cols in ((0, cols_f), (2, cols_g)):
                    cols[pl.ds(at, 8, stride=8), :] = flat[
                        pl.ds((zz * 2 + cc) * 32 + what + k, 8, stride=4), :
                    ]

    def product(a, b):
        return lax.dot_general(
            a,
            b,
            (((1,), (1,)), ((), ())),
            precision=lax.Precision.HIGHEST,
            preferred_element_type=jnp.float32,
        )

    part[:, 0:256] = product(rows_f[...], cols_f[...])
    part[:, 256:512] = product(rows_f[...], cols_g[...]) + product(rows_g[...], cols_f[...])

    def core_copy(i):
        block = y ^ i
        return pltpu.make_async_remote_copy(
            src_ref=part.at[pl.ds(pl.multiple_of((1 - core) * 128 + block * 16, 16), 16)],
            dst_ref=part_core.at[block],
            send_sem=core_out.at[i],
            recv_sem=core_in.at[i],
            device_id=place(x, y, z, 1 - core),
            device_id_type=MESH,
        )

    order = (1, 2, 3, 4, 5, 6, 7, 0)
    for i in order:
        core_copy(i).start()

    def ry_copy(i):
        return pltpu.make_async_remote_copy(
            src_ref=sums_y.at[y ^ i],
            dst_ref=part_y.at[y],
            send_sem=ry_out.at[i],
            recv_sem=ry_in.at[i],
            device_id=place(x, y ^ i, z, core),
            device_id_type=MESH,
        )

    for i in order:
        block = y ^ i
        core_copy(i).wait_recv()
        rows = pl.ds(pl.multiple_of(core * 128 + block * 16, 16), 16)
        sums_y[block] = part[rows, :] + part_core[block]
        if i:
            ry_copy(i).start()

    total = sums_y[y]
    for i in range(1, 8):
        ry_copy(i).wait_recv()
        total += part_y[y ^ i]

    for xx in range(8):
        c0, c1 = 32 * xx, 256 + 32 * xx
        sums_x[xx] = jnp.concatenate(
            [
                total[0:8, c0 : c0 + 32],
                total[8:16, c0 : c0 + 32],
                total[0:8, c1 : c1 + 32],
                total[8:16, c1 : c1 + 32],
            ],
            axis=1,
        )

    def rx_copy(i):
        return pltpu.make_async_remote_copy(
            src_ref=sums_x.at[x ^ i],
            dst_ref=part_x.at[x],
            send_sem=rx_out.at[i],
            recv_sem=rx_in.at[i],
            device_id=place(x ^ i, y, z, core),
            device_id_type=MESH,
        )

    for i in range(1, 8):
        rx_copy(i).start()
    tile = sums_x[x]
    for i in range(1, 8):
        rx_copy(i).wait_recv()
        tile += part_x[x ^ i]

    sums_z[...] = tile

    def rz_copy(i):
        return pltpu.make_async_remote_copy(
            src_ref=sums_z,
            dst_ref=part_z.at[z],
            send_sem=rz_out.at[i],
            recv_sem=rz_in.at[i],
            device_id=place(x, y, z ^ i, core),
            device_id_type=MESH,
        )

    for i in range(1, 8):
        rz_copy(i).start()
    for i in range(1, 8):
        rz_copy(i).wait_recv()
        tile += part_z[z ^ i]
    tile = pltpu.roll(tile, (128 - (zh // 2) * 32 - 16 * zl) % 128, 1)
    tile = pltpu.roll(tile, (zh % 2) * 4, 0) * (1.0 / CELLS)
    out_ref[0] = tile[0:4, 0:16]
    out_ref[1] = tile[0:4, 64:80]

    copies[0][0].wait_send()
    pots[0][0].wait_send()
    for mine in range(2):

        @pl.when(zl == mine)
        def _(mine=mine):
            for copy in outgoing(mine):
                copy.wait_send()

    for i in range(1, 8):
        y_copy(i).wait_send()
        ry_copy(i).wait_send()
        rx_copy(i).wait_send()
        rz_copy(i).wait_send()
    for i in range(1, 16):
        zc_copy(i).wait_send()
    for i in range(8):
        core_copy(i).wait_send()


def on_device(orbitals, potential):
    halves = orbitals.reshape(8, 2, 2, NY * NZ).transpose(1, 0, 2, 3).reshape(2, 16, NY * NZ)
    f32 = jnp.float32
    dma = pltpu.SemaphoreType.DMA
    vmem = pl.BlockSpec(memory_space=pltpu.VMEM)
    return pl.pallas_call(
        kernel,
        out_shape=jax.ShapeDtypeStruct((2, 4, 16), f32),
        in_specs=[vmem, vmem],
        out_specs=vmem,
        scratch_shapes=[
            pltpu.VMEM((96, NY * NZ), f32),
            pltpu.VMEM((48, NY * NZ), f32),
            pltpu.VMEM((96 * 8, 128), f32),
            pltpu.VMEM((FIRST * 16, 128), f32),
            pltpu.VMEM((SECOND * 16, 128), f32),
            pltpu.VMEM((48 * 8, 128), f32),
            pltpu.VMEM((8, 16, 4, 128), f32),
            pltpu.VMEM((8, 16, 4, 128), f32),
            pltpu.VMEM((128, 4, 128), f32),
            pltpu.VMEM((256, 128), f32),
            pltpu.VMEM((256, 128), f32),
            pltpu.VMEM((256, 128), f32),
            pltpu.VMEM((256, 128), f32),
            pltpu.VMEM((256, 512), f32),
            pltpu.VMEM((8, 16, 512), f32),
            pltpu.VMEM((8, 16, 512), f32),
            pltpu.VMEM((8, 16, 512), f32),
            pltpu.VMEM((8, 8, 128), f32),
            pltpu.VMEM((8, 8, 128), f32),
            pltpu.VMEM((8, 128), f32),
            pltpu.VMEM((8, 8, 128), f32),
            dma((16,)),
            dma((10,)),
            dma((8,)),
            dma((8,)),
            dma((16,)),
            dma((16,)),
            dma((8,)),
            dma((8,)),
            dma((8,)),
            dma((8,)),
            dma((8,)),
            dma((8,)),
            dma((8,)),
            dma((8,)),
        ],
        compiler_params=pltpu.CompilerParams(
            collective_id=0, has_side_effects=True, vmem_limit_bytes=32 * 1024 * 1024
        ),
        cost_estimate=pl.CostEstimate(
            flops=200_000_000, bytes_accessed=1_000_000, transcendentals=0
        ),
    )(halves, potential)


def solution(mesh):
    return jax.shard_map(
        on_device,
        mesh=mesh,
        in_specs=(P("dom", "orb", None), P("dom", None)),
        out_specs=P(None, "orb", "dom"),
        check_vma=False,
    )
```

time: 740 us -> 78.3 us (0.11); the launches traced: 729 us -> 78.1 us
  waiting for transfers between devices: 628 us -> 0 us
  Pallas kernels: 0 us -> 75.8 us
  starting transfers between devices: 54.5 us -> 0 us
  local copies, waits for them, and re-layouts: 24.2 us -> 2.3 us
  between operations: 14.6 us -> 0.04 us
    unnamed x4 -> x0, waiting for transfers between devices: 611 us -> none
    pallas_call x0 -> x1, Pallas kernels: none -> 75.8 us  [on_device(): pl.pallas_call(kernel, out_shape=jax.ShapeDtypeStruct((2, 4, 16), f32), i...]
    all_to_all x2 -> x0, starting transfers between devices: 29.3 us -> none  [the longest x1 24 us: on_device(): lax.all_to_all(following, 'orb', split_axis=2, concat_axis=1, tiled=True)]
    ppermute x6 -> x0, starting transfers between devices: 25.1 us -> none  [the longest x3 15.1 us: with_halo(): lax.ppermute(head, axis, [((i + 1) % count, i) for i in range(count)])]
    all_to_all x2 -> x0, waiting for transfers between devices: 14.1 us -> none  [the longest x1 7.45 us: on_device(): lax.all_to_all(following, 'orb', split_axis=2, concat_axis=1, tiled=True)]
    unnamed x17 -> x3, local copies, waits for them, and re-layouts: 14 us -> 1.25 us
  transfers between devices with their start and end apart: 10 -> 0, of which waited for: 7 -> 0; matrix products, arithmetic and copies ran while one was open for 2% -> 0% of each run, Pallas kernels for 0% -> 0%
where the time goes in v1:
time: 78.3 us; the launch traced here: 78.1 us
  Pallas kernels  75.8 us (97%)
  local copies, waits for them, and re-layouts  2.3 us (3%)
    pallas_call x1, Pallas kernels, on_device(): pl.pallas_call(kernel, out_shape=jax.ShapeDtypeStruct((2, 4, 16), f32), i...  75.8 us

profile of v1, /device:TPU:1, one launch (start us, length us, event | category | flops | bytes accessed | tf_op | source)
XLA Modules:
  0.0 78.1 jit_solution(4159228681217224714)
XLA Ops:
  0.0 1.0 %reshape.6 = f32[8,2,2,768]{3,2,1,0:T(2,128)S(1)} reshape(f32[8,4,768]{2,1,0:T(4,128)} %param.2) | data formatting | bytes 196608 | tf_op jit(solution)/shard_map/reshape | solution.py:457
  1.0 0.0 copy-start
  1.0 0.1 reshape.7.orb_ref
  1.1 0.7 copy-done
  1.7 75.8 %shard_map.28 = f32[2,4,16]{2,1,0:T(4,128)S(1)} custom-call(f32[2,16,768]{2,1,0:T(8,128)S(1)} %reshape.7.orb_ref, f32[8,768]{1,0:T(8,128)S(1)} %copy-done), custom_call_target="tpu_custom_call" | custom-call | flops 200000000 | bytes 1000000 | tf_op jit(solution)/shard_map/pallas_call | solution.py:461
  77.5 0.6 copy.7
  (1 shorter events, 0.0 us)
Async XLA Ops:
  1.0 0.7 copy-start

commit v2 on v1

v2 whole, which is shorter than its diff:
```python
import jax
import jax.numpy as jnp
from jax import lax
from jax.experimental import pallas as pl
from jax.experimental.pallas import tpu as pltpu
from jax.sharding import PartitionSpec as P

NZ = 96
NY = 8
CELLS = 98304
MESH = pl.DeviceIdType.MESH

coeffs = (
    -5369.0 / 1800.0,
    12.0 / 7.0,
    -15.0 / 56.0,
    10.0 / 189.0,
    -1.0 / 112.0,
    2.0 / 1925.0,
    -1.0 / 16632.0,
)
CENTER = 6.5
HALF = 6.5


def place(x, y, z, core):
    return {"dom": x * 2 + z % 2, "orb": (z // 2) * 16 + y * 2 + core}


def distance(shape, axis):
    return lax.broadcasted_iota(jnp.int32, shape, axis)


def band_x(rows, columns, offset, both):
    gap = distance((rows, columns), 1) - distance((rows, columns), 0) - offset
    band = jnp.zeros((rows, columns), jnp.float32)
    for j in range(1, 7):
        if both:
            band = jnp.where((gap == 2 * j) | (gap == -2 * j), coeffs[j], band)
        else:
            band = jnp.where(gap == 2 * j, 2.0 * coeffs[j], band)
    return band


def band_z():
    rows, columns = distance((128, 128), 0), distance((128, 128), 1)
    gap = rows - columns
    inside = (rows < NZ) & (columns < NZ)
    band = jnp.zeros((128, 128), jnp.float32)
    for j in range(1, 7):
        near = (gap == j) | (gap == -j) | (gap == NZ - j) | (gap == j - NZ)
        band = jnp.where(near & inside, coeffs[j], band)
    return band


def dot(a, b):
    return lax.dot_general(
        a,
        b,
        (((1,), (0,)), ((), ())),
        precision=lax.Precision.HIGHEST,
        preferred_element_type=jnp.float32,
    )


def dot_t(a, b):
    return lax.dot_general(
        a,
        b,
        (((1,), (1,)), ((), ())),
        precision=lax.Precision.HIGHEST,
        preferred_element_type=jnp.float32,
    )


def kernel(
    orb_ref,
    pot_ref,
    out_ref,
    raw,
    raw_pot,
    field0,
    field1,
    field2,
    poten,
    x_one,
    x_two,
    x_three,
    z_all,
    sum_x,
    sum_z,
    send_f,
    send_g,
    mid_f,
    mid_g,
    last_f,
    last_g,
    rows_f,
    rows_g,
    cols_f,
    cols_g,
    corr,
    proj,
    corr_core,
    proj_core,
    corr_one,
    proj_one,
    corr_got,
    proj_got,
    corr_two,
    proj_two,
    corr_have,
    proj_have,
    sums_z,
    part_z,
    halo_out,
    halo_in,
    own_in,
    f_out,
    f_in,
    g_out,
    g_in,
    f2_out,
    f2_in,
    g2_out,
    g2_in,
    ca_out,
    ca_in,
    cb_out,
    cb_in,
    ra_out,
    ra_in,
    rb_out,
    rb_in,
    sa_out,
    sa_in,
    sb_out,
    sb_in,
    rz_out,
    rz_in,
):
    dom = lax.axis_index("dom")
    orb = lax.axis_index("orb")
    x, zl = dom // 2, dom % 2
    core, y, zh = orb % 2, (orb // 2) % 8, orb // 16
    z = zh * 2 + zl
    zc = z * 2 + core
    right, left = (x + 1) % 8, (x + 7) % 8
    right2, left2 = (x + 2) % 8, (x + 6) % 8
    pair = z + 1 - 2 * zl
    z0 = zh * 2

    raw[pl.ds(92, 4), :] = jnp.zeros((4, NY * NZ), jnp.float32)
    barrier = pltpu.get_barrier_semaphore()

    def greet(device):
        pl.semaphore_signal(barrier, inc=1, device_id=device, device_id_type=MESH)

    for i in range(1, 8):
        greet(place(x, y ^ i, z, core))
        greet(place(x ^ i, y, z, core))
    for i in range(1, 16):
        other = zc ^ i
        greet(place(x, y, other // 2, other % 2))
    greet(place(right, y, pair, core))
    greet(place(left, y, pair, core))

    @pl.when(zl == 1)
    def _():
        greet(place(right2, y, pair, core))

    own_row = pl.multiple_of(24 + 16 * zl, 8)
    raw[pl.ds(own_row, 16), :] = orb_ref[zl]
    own_pot = pl.multiple_of(16 + 8 * zl, 8)
    raw_pot[pl.ds(own_pot, 8), :] = pot_ref[...]

    x_one[...] = band_x(72, 96, 8, True)
    x_two[...] = band_x(48, 72, 16, True)
    x_three[...] = band_x(32, 48, 0, False)
    z_all[...] = band_z()

    def spread(start, blocks):
        def step(block, _):
            row = pl.multiple_of(start + block * 8, 8)
            for yy in range(NY):
                tile = raw[pl.ds(row, 8), NZ * yy : NZ * yy + NZ]
                tile = jnp.concatenate([tile, jnp.zeros((8, 32), jnp.float32)], axis=1)
                field0[pl.ds(row, 8), 128 * yy : 128 * yy + 128] = tile
            return 0

        lax.fori_loop(0, blocks, step, 0)

    def spread_pot(row):
        for yy in range(NY):
            tile = raw_pot[pl.ds(row, 8), NZ * yy : NZ * yy + NZ]
            tile = jnp.concatenate([tile, jnp.zeros((8, 32), jnp.float32)], axis=1)
            for k in range(2):
                poten[yy, pl.ds(row * 2 + k, 8, stride=2), :] = tile

    spread(own_row, 2)
    spread_pot(own_pot)
    pl.semaphore_wait(barrier, 32 - zl)

    def orb_copy(half, start, count, row, slot, device):
        return pltpu.make_async_remote_copy(
            src_ref=orb_ref.at[half, pl.ds(start, count)],
            dst_ref=raw.at[pl.ds(row, count)],
            send_sem=halo_out.at[slot],
            recv_sem=halo_in.at[slot],
            device_id=device,
            device_id_type=MESH,
        )

    def pot_copy(row, slot, device, out_slot):
        return pltpu.make_async_remote_copy(
            src_ref=pot_ref,
            dst_ref=raw_pot.at[pl.ds(row, 8)],
            send_sem=halo_out.at[out_slot],
            recv_sem=halo_in.at[slot],
            device_id=device,
            device_id_type=MESH,
        )

    copies = [(orb_copy(1 - zl, 0, 16, own_row, 0, place(x, y, pair, core)), None)]
    pots = [(pot_copy(own_pot, 6, place(x, y, pair, core), 8), None)]
    for t in range(2):
        to_left = place(left, y, z0 + t, core)
        to_right = place(right, y, z0 + t, core)
        to_left2 = place(left2, y, z0 + t, core)
        for mine in range(2):
            row = 56 + 16 * mine
            slot = 1 + mine
            copies.append((to_left, t, mine, 0, 16, row, slot))
            pots.append((to_left, mine, 32 + 8 * mine, 7 + mine))
        copies.append((to_right, t, 0, 8, 8, 0, 4))
        copies.append((to_right, t, 1, 0, 16, 8, 5))
        pots.append((to_right, 1, 8, 9))
        copies.append((to_left2, t, 0, 0, 4, 88, 3))

    copies[0][0].start()
    pots[0][0].start()

    def guarded(mine, action):
        pl.when(zl == mine)(action)

    def outgoing(mine):
        result = []
        at = 1
        for device, t, who, start, count, row, slot in copies[1:]:
            if who == mine:
                result.append(
                    pltpu.make_async_remote_copy(
                        src_ref=orb_ref.at[t, pl.ds(start, count)],
                        dst_ref=raw.at[pl.ds(row, count)],
                        send_sem=halo_out.at[at],
                        recv_sem=halo_in.at[slot],
                        device_id=device,
                        device_id_type=MESH,
                    )
                )
                at += 1
        at = 9
        for device, who, row, slot in pots[1:]:
            if who == mine:
                result.append(pot_copy(row, slot, device, at))
                at += 1
        return result

    for mine in range(2):

        @pl.when(zl == mine)
        def _(mine=mine):
            for copy in outgoing(mine):
                copy.start()

    me = place(x, y, pair, core)
    pair_row = pl.multiple_of(40 - 16 * zl, 8)
    pair_pot = pl.multiple_of(24 - 8 * zl, 8)
    orb_copy(0, 0, 16, pair_row, 0, me).wait_recv()
    spread(pair_row, 2)
    orb_copy(0, 0, 16, 56, 1, me).wait_recv()
    orb_copy(0, 0, 16, 72, 2, me).wait_recv()
    spread(56, 4)
    orb_copy(0, 8, 8, 0, 4, me).wait_recv()
    orb_copy(0, 0, 16, 8, 5, me).wait_recv()
    spread(0, 3)
    orb_copy(0, 0, 4, 88, 3, me).wait_recv()
    spread(88, 1)
    pot_copy(pair_pot, 6, me, 8).wait_recv()
    spread_pot(pair_pot)
    for slot, row in ((7, 32), (8, 40), (9, 8)):
        pot_copy(row, slot, me, 8).wait_recv()
        spread_pot(row)

    def columns(yy):
        return slice(128 * (yy % NY), 128 * (yy % NY) + 128)

    def apply(field, start, count, band, pot_row, scale, diagonal, finish):
        rows = slice(start, start + count)
        sum_x[0:count, :] = dot(band[...], field[...])
        stacked = jnp.concatenate([field[rows, columns(yy)] for yy in range(NY)], axis=0)
        sum_z[0 : count * NY, :] = dot(stacked, z_all[...])
        for yy in range(NY):
            here = field[rows, columns(yy)]
            total = sum_x[0:count, columns(yy)] + sum_z[count * yy : count * yy + count, :]
            total += coeffs[1] * (field[rows, columns(yy + 1)] + field[rows, columns(yy + 7)])
            total += (coeffs[2] + coeffs[6]) * (
                field[rows, columns(yy + 2)] + field[rows, columns(yy + 6)]
            )
            total += (coeffs[3] + coeffs[5]) * (
                field[rows, columns(yy + 3)] + field[rows, columns(yy + 5)]
            )
            total += (2.0 * coeffs[4]) * field[rows, columns(yy + 4)]
            weight = poten[yy, pot_row : pot_row + count, :] * diagonal[0] + diagonal[1]
            finish(yy, scale * total + weight * here)

    level = -1.5 * coeffs[0]

    def first(yy, value):
        field1[:, columns(yy)] = value

    apply(
        field0, 8, 72, x_one, 16, -0.5 / HALF, (1.0 / HALF, (level - CENTER) / HALF), first
    )

    def second(yy, value):
        value -= field0[24:72, columns(yy)]
        field2[:, columns(yy)] = value
        send_f[yy] = value[0:32]

    apply(
        field1,
        16,
        48,
        x_two,
        32,
        -1.0 / HALF,
        (2.0 / HALF, 2.0 * (level - CENTER) / HALF),
        second,
    )

    def f_copy(i):
        return pltpu.make_async_remote_copy(
            src_ref=send_f.at[y ^ i],
            dst_ref=mid_f.at[y],
            send_sem=f_out.at[i],
            recv_sem=f_in.at[i],
            device_id=place(x, y ^ i, z, core),
            device_id_type=MESH,
        )

    for i in range(1, 8):
        f_copy(i).start()
    mid_f[y] = send_f[y]

    def third(yy, value):
        send_g[yy] = value

    apply(field2, 0, 32, x_three, 32, -0.25, (0.5, 0.5 * level), third)

    def plane_of(ref, index):
        return ref.at[:, pl.ds(index * 2, 2)]

    def g_copy(i):
        other = zc ^ i
        return pltpu.make_async_remote_copy(
            src_ref=plane_of(send_g, other),
            dst_ref=plane_of(mid_g, zc),
            send_sem=g_out.at[i],
            recv_sem=g_in.at[i],
            device_id=place(x, y, other // 2, other % 2),
            device_id_type=MESH,
        )

    for i in range(1, 16):
        g_copy(i).start()
    own_g = pltpu.make_async_copy(plane_of(send_g, zc), plane_of(mid_g, zc), own_in.at[0])
    own_g.start()

    def f2_copy(i):
        other = zc ^ i
        return pltpu.make_async_remote_copy(
            src_ref=plane_of(mid_f, other),
            dst_ref=plane_of(last_f, zc),
            send_sem=f2_out.at[i],
            recv_sem=f2_in.at[i],
            device_id=place(x, y, other // 2, other % 2),
            device_id_type=MESH,
        )

    def g2_copy(i):
        return pltpu.make_async_remote_copy(
            src_ref=mid_g.at[y ^ i],
            dst_ref=last_g.at[y],
            send_sem=g2_out.at[i],
            recv_sem=g2_in.at[i],
            device_id=place(x, y ^ i, z, core),
            device_id_type=MESH,
        )

    for i in range(1, 8):
        f_copy(i).wait_recv()
    for i in range(1, 16):
        f2_copy(i).start()
    own_f = pltpu.make_async_copy(plane_of(mid_f, zc), plane_of(last_f, zc), own_in.at[1])
    own_f.start()
    own_g.wait()
    for i in range(1, 16):
        g_copy(i).wait_recv()
    for i in range(1, 8):
        g2_copy(i).start()
    last_g[y] = mid_g[y]

    def reorder(last, rows, cols):
        flat = last.reshape(256, 128)
        for yy in range(8):
            for cc in range(2):
                for k in range(2):
                    rows[pl.ds((cc * 8 + yy) * 16 + k, 8, stride=2), :] = flat[
                        pl.ds(yy * 32 + cc * 2 + k, 8, stride=4), :
                    ]
        for zz in range(8):
            for cc in range(2):
                for k in range(2):
                    cols[pl.ds((zz // 2) * 64 + cc * 4 + (zz % 2) * 2 + k, 8, stride=8), :] = flat[
                        pl.ds(zz * 4 + cc * 2 + k, 8, stride=32), :
                    ]

    own_f.wait()
    for i in range(1, 16):
        f2_copy(i).wait_recv()
    reorder(last_f, rows_f, cols_f)
    corr[...] = dot_t(rows_f[...], cols_f[...])

    order = (1, 2, 3, 4, 5, 6, 7, 0)

    def ca_copy(i):
        block = y ^ i
        return pltpu.make_async_remote_copy(
            src_ref=corr.at[pl.ds(pl.multiple_of((1 - core) * 128 + block * 16, 16), 16)],
            dst_ref=corr_core.at[block],
            send_sem=ca_out.at[i],
            recv_sem=ca_in.at[i],
            device_id=place(x, y, z, 1 - core),
            device_id_type=MESH,
        )

    def cb_copy(i):
        block = x ^ i
        return pltpu.make_async_remote_copy(
            src_ref=proj.at[1 - core, pl.ds(pl.multiple_of(block * 32, 32), 32)],
            dst_ref=proj_core.at[block],
            send_sem=cb_out.at[i],
            recv_sem=cb_in.at[i],
            device_id=place(x, y, z, 1 - core),
            device_id_type=MESH,
        )

    def ra_copy(i):
        return pltpu.make_async_remote_copy(
            src_ref=corr_one.at[y ^ i],
            dst_ref=corr_got.at[y],
            send_sem=ra_out.at[i],
            recv_sem=ra_in.at[i],
            device_id=place(x, y ^ i, z, core),
            device_id_type=MESH,
        )

    def rb_copy(i):
        return pltpu.make_async_remote_copy(
            src_ref=proj_one.at[x ^ i],
            dst_ref=proj_got.at[x],
            send_sem=rb_out.at[i],
            recv_sem=rb_in.at[i],
            device_id=place(x ^ i, y, z, core),
            device_id_type=MESH,
        )

    for i in order:
        ca_copy(i).start()
    for i in range(1, 8):
        g2_copy(i).wait_recv()
    reorder(last_g, rows_g, cols_g)
    both = dot_t(cols_f[...], rows_g[...]) + dot_t(cols_g[...], rows_f[...])
    proj[0] = both[:, 0:128]
    proj[1] = both[:, 128:256]
    for i in order:
        cb_copy(i).start()
    for i in order:
        block = y ^ i
        ca_copy(i).wait_recv()
        rows = pl.ds(pl.multiple_of(core * 128 + block * 16, 16), 16)
        corr_one[block] = corr[rows, :] + corr_core[block]
        if i:
            ra_copy(i).start()
    for i in order:
        block = x ^ i
        cb_copy(i).wait_recv()
        rows = pl.ds(pl.multiple_of(block * 32, 32), 32)
        proj_one[block] = proj[core, rows, :] + proj_core[block]
        if i:
            rb_copy(i).start()

    def sa_copy(i):
        return pltpu.make_async_remote_copy(
            src_ref=corr_two.at[x ^ i],
            dst_ref=corr_have.at[x],
            send_sem=sa_out.at[i],
            recv_sem=sa_in.at[i],
            device_id=place(x ^ i, y, z, core),
            device_id_type=MESH,
        )

    def sb_copy(i):
        return pltpu.make_async_remote_copy(
            src_ref=proj_two.at[y ^ i],
            dst_ref=proj_have.at[y],
            send_sem=sb_out.at[i],
            recv_sem=sb_in.at[i],
            device_id=place(x, y ^ i, z, core),
            device_id_type=MESH,
        )

    blank = jnp.zeros((8, 64), jnp.float32)
    total = corr_one[y]
    for i in range(1, 8):
        ra_copy(i).wait_recv()
        total += corr_got[y ^ i]
    for xx in range(8):
        at = slice(32 * xx, 32 * xx + 32)
        corr_two[xx] = jnp.concatenate([total[0:8, at], total[8:16, at], blank], axis=1)
    for i in range(1, 8):
        sa_copy(i).start()
    total = proj_one[x]
    for i in range(1, 8):
        rb_copy(i).wait_recv()
        total += proj_got[x ^ i]
    for yy in range(8):
        at = slice(16 * yy, 16 * yy + 16)
        proj_two[yy] = jnp.concatenate(
            [total[8 * b : 8 * b + 8, at] for b in range(4)] + [blank], axis=1
        )
    for i in range(1, 8):
        sb_copy(i).start()
    one = corr_two[x]
    for i in range(1, 8):
        sa_copy(i).wait_recv()
        one += corr_have[x ^ i]
    two = proj_two[y]
    for i in range(1, 8):
        sb_copy(i).wait_recv()
        two += proj_have[y ^ i]
    tile = one + pltpu.roll(two, 64, 1)

    sums_z[...] = tile

    def rz_copy(i):
        return pltpu.make_async_remote_copy(
            src_ref=sums_z,
            dst_ref=part_z.at[z],
            send_sem=rz_out.at[i],
            recv_sem=rz_in.at[i],
            device_id=place(x, y, z ^ i, core),
            device_id_type=MESH,
        )

    for i in range(1, 8):
        rz_copy(i).start()
    for i in range(1, 8):
        rz_copy(i).wait_recv()
        tile += part_z[z ^ i]
    tile = tile * (1.0 / CELLS)
    one = pltpu.roll(tile, (128 - (zh // 2) * 32 - 16 * zl) % 128, 1)
    out_ref[0] = pltpu.roll(one, (zh % 2) * 4, 0)[0:4, 0:16]
    two = pltpu.roll(tile, 64 - 32 * zl - 4 * zh, 1).T
    out_ref[1] = jnp.concatenate([two[0:4, :], two[16:20, :]], axis=1)

    copies[0][0].wait_send()
    pots[0][0].wait_send()
    for mine in range(2):

        @pl.when(zl == mine)
        def _(mine=mine):
            for copy in outgoing(mine):
                copy.wait_send()

    for i in range(1, 8):
        for copy in (f_copy, g2_copy, ra_copy, rb_copy, sa_copy, sb_copy, rz_copy):
            copy(i).wait_send()
    for i in range(1, 16):
        g_copy(i).wait_send()
        f2_copy(i).wait_send()
    for i in range(8):
        ca_copy(i).wait_send()
        cb_copy(i).wait_send()


def on_device(orbitals, potential):
    halves = orbitals.reshape(8, 2, 2, NY * NZ).transpose(1, 0, 2, 3).reshape(2, 16, NY * NZ)
    f32 = jnp.float32
    vmem = pl.BlockSpec(memory_space=pltpu.VMEM)
    buffers = (
        [(96, 768), (48, 768), (96, 1024), (72, 1024), (48, 1024), (8, 96, 128)]
        + [(72, 96), (48, 72), (32, 48), (128, 128), (72, 1024), (576, 128)]
        + [(8, 32, 128)] * 6
        + [(256, 128)] * 4
        + [(256, 256), (2, 256, 128)]
        + [(8, 16, 256), (8, 32, 128)] * 3
        + [(8, 8, 128)] * 4
        + [(8, 128), (8, 8, 128)]
    )
    sems = [16, 10, 2] + [8, 8, 16, 16, 16, 16, 8, 8] + [8] * 14
    return pl.pallas_call(
        kernel,
        out_shape=jax.ShapeDtypeStruct((2, 4, 16), f32),
        in_specs=[vmem, vmem],
        out_specs=vmem,
        scratch_shapes=[pltpu.VMEM(shape, f32) for shape in buffers]
        + [pltpu.SemaphoreType.DMA((count,)) for count in sems],
        compiler_params=pltpu.CompilerParams(
            collective_id=0, has_side_effects=True, vmem_limit_bytes=32 * 1024 * 1024
        ),
        cost_estimate=pl.CostEstimate(
            flops=200_000_000, bytes_accessed=1_000_000, transcendentals=0
        ),
    )(halves, potential)


def solution(mesh):
    return jax.shard_map(
        on_device,
        mesh=mesh,
        in_specs=(P("dom", "orb", None), P("dom", None)),
        out_specs=P(None, "orb", "dom"),
        check_vma=False,
    )
```

time: 78.3 us -> 64.9 us (0.83)
  Pallas kernels: 75.8 us -> 62.3 us
    pallas_call x1, Pallas kernels: 75.8 us -> 62.3 us  [on_device(): pl.pallas_call(kernel, out_shape=jax.ShapeDtypeStruct((2, 4, 16), f32), i...]
where the time goes in v2:
time: 64.9 us; the launch traced here: 64.6 us
  Pallas kernels  62.3 us (96%)
  local copies, waits for them, and re-layouts  2.3 us (4%)
    pallas_call x1, Pallas kernels, on_device(): pl.pallas_call(kernel, out_shape=jax.ShapeDtypeStruct((2, 4, 16), f32), i...  62.3 us

profile of v2, /device:TPU:1, one launch (start us, length us, event | category | flops | bytes accessed | tf_op | source)
XLA Modules:
  0.0 64.6 jit_solution(13337759791570517644)
XLA Ops:
  0.0 1.0 %reshape.6 = f32[8,2,2,768]{3,2,1,0:T(2,128)S(1)} reshape(f32[8,4,768]{2,1,0:T(4,128)} %param.2) | data formatting | bytes 196608 | tf_op jit(solution)/shard_map/reshape | solution.py:599
  1.0 0.0 copy-start
  1.0 0.1 reshape.7.orb_ref
  1.1 0.7 %copy-done = f32[8,768]{1,0:T(8,128)S(1)} copy-done((f32[8,768]{1,0:T(8,128)S(1)}, f32[8,768]{1,0:T(8,128)}, u32[]{:S(2)}) %copy-start) | copy-done | bytes 24600
  1.7 62.3 %shard_map.28 = f32[2,4,16]{2,1,0:T(4,128)S(1)} custom-call(f32[2,16,768]{2,1,0:T(8,128)S(1)} %reshape.7.orb_ref, f32[8,768]{1,0:T(8,128)S(1)} %copy-done), custom_call_target="tpu_custom_call" | custom-call | flops 200000000 | bytes 1000000 | tf_op jit(solution)/shard_map/pallas_call | solution.py:613
  64.0 0.6 copy.7
  (1 shorter events, 0.0 us)
Async XLA Ops:
  1.0 0.7 %copy-start = (f32[8,768]{1,0:T(8,128)S(1)}, f32[8,768]{1,0:T(8,128)}, u32[]{:S(2)}) copy-start(f32[8,768]{1,0:T(8,128)} %pot_ref.1) | copy-start | bytes 73732

commit v3 on v2

--- a/solution.py
+++ b/solution.py
@@ -22,6 +22,9 @@
 CENTER = 6.5
 HALF = 6.5
 
+FAR = (4, 3, 5, 2, 6, 1, 7)
+FAR_PAIRS = tuple(2 * d + flip for d in FAR for flip in range(2)) + (1,)
+
 
 def place(x, y, z, core):
     return {"dom": x * 2 + z % 2, "orb": (z // 2) * 16 + y * 2 + core}
@@ -43,13 +46,13 @@
 
 
 def band_z():
-    rows, columns = distance((128, 128), 0), distance((128, 128), 1)
+    rows, columns = distance((256, 256), 0), distance((256, 256), 1)
     gap = rows - columns
-    inside = (rows < NZ) & (columns < NZ)
-    band = jnp.zeros((128, 128), jnp.float32)
+    same = (rows // 128 == columns // 128) & (rows % 128 < NZ) & (columns % 128 < NZ)
+    band = jnp.zeros((256, 256), jnp.float32)
     for j in range(1, 7):
         near = (gap == j) | (gap == -j) | (gap == NZ - j) | (gap == j - NZ)
-        band = jnp.where(near & inside, coeffs[j], band)
+        band = jnp.where(near & same, coeffs[j], band)
     return band
 
 
@@ -74,9 +77,12 @@
 
 
 def kernel(
+    orb_hbm,
+    pot_hbm,
+    out_ref,
+    orb_raw,
     orb_ref,
     pot_ref,
-    out_ref,
     raw,
     raw_pot,
     field0,
@@ -95,6 +101,9 @@
     mid_g,
     last_f,
     last_g,
+    turn_f,
+    turn_g,
+    back_g,
     rows_f,
     rows_g,
     cols_f,
@@ -138,6 +147,7 @@
     sb_in,
     rz_out,
     rz_in,
+    near,
 ):
     dom = lax.axis_index("dom")
     orb = lax.axis_index("orb")
@@ -151,25 +161,50 @@
     z0 = zh * 2
 
     raw[pl.ds(92, 4), :] = jnp.zeros((4, NY * NZ), jnp.float32)
+    load_orb = pltpu.make_async_copy(orb_hbm, orb_raw, own_in.at[2])
+    load_pot = pltpu.make_async_copy(pot_hbm, pot_ref, own_in.at[3])
+    load_orb.start()
+    load_pot.start()
     barrier = pltpu.get_barrier_semaphore()
 
     def greet(device):
         pl.semaphore_signal(barrier, inc=1, device_id=device, device_id_type=MESH)
 
-    for i in range(1, 8):
-        greet(place(x, y ^ i, z, core))
-        greet(place(x ^ i, y, z, core))
-    for i in range(1, 16):
-        other = zc ^ i
-        greet(place(x, y, other // 2, other % 2))
+    steps = (
+        lambda d: place((x + d) % 8, y, z, core),
+        lambda d: place(x, (y + d) % 8, z, core),
+        lambda d: place(x, y, (z + d) % 8, core),
+    )
+    greet(place(right2, y, z0, core))
     greet(place(right, y, pair, core))
     greet(place(left, y, pair, core))
-
-    @pl.when(zl == 1)
-    def _():
-        greet(place(right2, y, pair, core))
+    for step in steps:
+        greet(step(1))
+        greet(step(7))
+    greet(place(x, y, z, 1 - core))
+
+    def tell(turn):
+        for axis, step in enumerate(steps):
+            for side in range(2):
+                pl.semaphore_signal(
+                    near.at[axis, side, turn],
+                    inc=1,
+                    device_id=step(7 if side else 1),
+                    device_id_type=MESH,
+                )
+
+    def hear(turn):
+        for axis in range(3):
+            for side in range(2):
+                pl.semaphore_wait(near.at[axis, side, turn], 1)
 
     own_row = pl.multiple_of(24 + 16 * zl, 8)
+    load_orb.wait()
+    for p in range(8):
+        four = orb_raw[p]
+        orb_ref[0, 2 * p : 2 * p + 2, :] = four[0:2]
+        orb_ref[1, 2 * p : 2 * p + 2, :] = four[2:4]
+    load_pot.wait()
     raw[pl.ds(own_row, 16), :] = orb_ref[zl]
     own_pot = pl.multiple_of(16 + 8 * zl, 8)
     raw_pot[pl.ds(own_pot, 8), :] = pot_ref[...]
@@ -199,7 +234,7 @@
 
     spread(own_row, 2)
     spread_pot(own_pot)
-    pl.semaphore_wait(barrier, 32 - zl)
+    pl.semaphore_wait(barrier, 11 - 2 * zl)
 
     def orb_copy(half, start, count, row, slot, device):
         return pltpu.make_async_remote_copy(
@@ -273,17 +308,24 @@
             for copy in outgoing(mine):
                 copy.start()
 
+    tell(0)
     me = place(x, y, pair, core)
     pair_row = pl.multiple_of(40 - 16 * zl, 8)
     pair_pot = pl.multiple_of(24 - 8 * zl, 8)
     orb_copy(0, 0, 16, pair_row, 0, me).wait_recv()
     spread(pair_row, 2)
+    hear(0)
+    tell(1)
     orb_copy(0, 0, 16, 56, 1, me).wait_recv()
     orb_copy(0, 0, 16, 72, 2, me).wait_recv()
     spread(56, 4)
+    hear(1)
+    tell(2)
     orb_copy(0, 8, 8, 0, 4, me).wait_recv()
     orb_copy(0, 0, 16, 8, 5, me).wait_recv()
     spread(0, 3)
+    hear(2)
+    tell(3)
     orb_copy(0, 0, 4, 88, 3, me).wait_recv()
     spread(88, 1)
     pot_copy(pair_pot, 6, me, 8).wait_recv()
@@ -292,17 +334,20 @@
         pot_copy(row, slot, me, 8).wait_recv()
         spread_pot(row)
 
+    hear(3)
+
     def columns(yy):
         return slice(128 * (yy % NY), 128 * (yy % NY) + 128)
 
     def apply(field, start, count, band, pot_row, scale, diagonal, finish):
         rows = slice(start, start + count)
         sum_x[0:count, :] = dot(band[...], field[...])
-        stacked = jnp.concatenate([field[rows, columns(yy)] for yy in range(NY)], axis=0)
-        sum_z[0 : count * NY, :] = dot(stacked, z_all[...])
+        stacked = jnp.concatenate([field[rows, 256 * q : 256 * q + 256] for q in range(4)], axis=0)
+        sum_z[0 : count * 4, :] = dot(stacked, z_all[...])
         for yy in range(NY):
             here = field[rows, columns(yy)]
-            total = sum_x[0:count, columns(yy)] + sum_z[count * yy : count * yy + count, :]
+            q, half = yy // 2, columns(yy % 2)
+            total = sum_x[0:count, columns(yy)] + sum_z[count * q : count * q + count, half]
             total += coeffs[1] * (field[rows, columns(yy + 1)] + field[rows, columns(yy + 7)])
             total += (coeffs[2] + coeffs[6]) * (
                 field[rows, columns(yy + 2)] + field[rows, columns(yy + 6)]
@@ -341,15 +386,15 @@
 
     def f_copy(i):
         return pltpu.make_async_remote_copy(
-            src_ref=send_f.at[y ^ i],
+            src_ref=send_f.at[(y + i) % 8],
             dst_ref=mid_f.at[y],
             send_sem=f_out.at[i],
             recv_sem=f_in.at[i],
-            device_id=place(x, y ^ i, z, core),
-            device_id_type=MESH,
-        )
-
-    for i in range(1, 8):
+            device_id=place(x, (y + i) % 8, z, core),
+            device_id_type=MESH,
+        )
+
+    for i in FAR:
         f_copy(i).start()
     mid_f[y] = send_f[y]
 
@@ -358,30 +403,45 @@
 
     apply(field2, 0, 32, x_three, 32, -0.25, (0.5, 0.5 * level), third)
 
-    def plane_of(ref, index):
-        return ref.at[:, pl.ds(index * 2, 2)]
+    def by_plane(source, target):
+        source, target = source.reshape(256, 128), target.reshape(256, 128)
+        for p in range(16):
+            for k in range(2):
+                target[pl.ds(p * 16 + k, 8, stride=2), :] = source[
+                    pl.ds(p * 2 + k, 8, stride=32), :
+                ]
+
+    def by_row(source, target):
+        source, target = source.reshape(256, 128), target.reshape(256, 128)
+        for yy in range(8):
+            for p in (0, 8):
+                for k in range(2):
+                    target[pl.ds(yy * 32 + p * 2 + k, 8, stride=2), :] = source[
+                        pl.ds(p * 16 + yy * 2 + k, 8, stride=16), :
+                    ]
+
+    by_plane(send_g, turn_g)
 
     def g_copy(i):
-        other = zc ^ i
-        return pltpu.make_async_remote_copy(
-            src_ref=plane_of(send_g, other),
-            dst_ref=plane_of(mid_g, zc),
+        other = ((z + i // 2) % 8) * 2 + core + (i % 2) * (1 - 2 * core)
+        return pltpu.make_async_remote_copy(
+            src_ref=turn_g.at[other],
+            dst_ref=mid_g.at[zc],
             send_sem=g_out.at[i],
             recv_sem=g_in.at[i],
             device_id=place(x, y, other // 2, other % 2),
             device_id_type=MESH,
         )
 
-    for i in range(1, 16):
+    for i in FAR_PAIRS:
         g_copy(i).start()
-    own_g = pltpu.make_async_copy(plane_of(send_g, zc), plane_of(mid_g, zc), own_in.at[0])
-    own_g.start()
+    mid_g[zc] = turn_g[zc]
 
     def f2_copy(i):
-        other = zc ^ i
-        return pltpu.make_async_remote_copy(
-            src_ref=plane_of(mid_f, other),
-            dst_ref=plane_of(last_f, zc),
+        other = ((z + i // 2) % 8) * 2 + core + (i % 2) * (1 - 2 * core)
+        return pltpu.make_async_remote_copy(
+            src_ref=turn_f.at[other],
+            dst_ref=last_f.at[zc],
             send_sem=f2_out.at[i],
             recv_sem=f2_in.at[i],
             device_id=place(x, y, other // 2, other % 2),
@@ -390,52 +450,63 @@
 
     def g2_copy(i):
         return pltpu.make_async_remote_copy(
-            src_ref=mid_g.at[y ^ i],
+            src_ref=back_g.at[(y + i) % 8],
             dst_ref=last_g.at[y],
             send_sem=g2_out.at[i],
             recv_sem=g2_in.at[i],
-            device_id=place(x, y ^ i, z, core),
-            device_id_type=MESH,
-        )
-
-    for i in range(1, 8):
+            device_id=place(x, (y + i) % 8, z, core),
+            device_id_type=MESH,
+        )
+
+    for i in FAR[::-1]:
         f_copy(i).wait_recv()
-    for i in range(1, 16):
+    by_plane(mid_f, turn_f)
+    for i in FAR_PAIRS:
         f2_copy(i).start()
-    own_f = pltpu.make_async_copy(plane_of(mid_f, zc), plane_of(last_f, zc), own_in.at[1])
-    own_f.start()
-    own_g.wait()
+    last_f[zc] = turn_f[zc]
     for i in range(1, 16):
         g_copy(i).wait_recv()
+    by_row(mid_g, back_g)
+    for i in FAR:
+        g2_copy(i).start()
+    last_g[y] = back_g[y]
+
+    def reorder(last, rows, cols, along_z, along_c, along_y):
+        flat = last.reshape(256, 128)
+        for cc in range(2):
+            for k in range(2):
+                for yy in range(8):
+                    rows[pl.ds((cc * 8 + yy) * 16 + k, 8, stride=2), :] = flat[
+                        pl.ds(yy * along_y + cc * along_c + k, 8, stride=along_z), :
+                    ]
+                for zz in range(8):
+                    at = (zz // 2) * 64 + cc * 4 + (zz % 2) * 2 + k
+                    cols[pl.ds(at, 8, stride=8), :] = flat[
+                        pl.ds(zz * along_z + cc * along_c + k, 8, stride=along_y), :
+                    ]
+
+    copies[0][0].wait_send()
+    pots[0][0].wait_send()
+    for mine in range(2):
+
+        @pl.when(zl == mine)
+        def _(mine=mine):
+            for copy in outgoing(mine):
+                copy.wait_send()
+
     for i in range(1, 8):
-        g2_copy(i).start()
-    last_g[y] = mid_g[y]
-
-    def reorder(last, rows, cols):
-        flat = last.reshape(256, 128)
-        for yy in range(8):
-            for cc in range(2):
-                for k in range(2):
-                    rows[pl.ds((cc * 8 + yy) * 16 + k, 8, stride=2), :] = flat[
-                        pl.ds(yy * 32 + cc * 2 + k, 8, stride=4), :
-                    ]
-        for zz in range(8):
-            for cc in range(2):
-                for k in range(2):
-                    cols[pl.ds((zz // 2) * 64 + cc * 4 + (zz % 2) * 2 + k, 8, stride=8), :] = flat[
-                        pl.ds(zz * 4 + cc * 2 + k, 8, stride=32), :
-                    ]
-
-    own_f.wait()
+        f_copy(i).wait_send()
+    for i in range(1, 16):
+        g_copy(i).wait_send()
     for i in range(1, 16):
         f2_copy(i).wait_recv()
-    reorder(last_f, rows_f, cols_f)
+    reorder(last_f, rows_f, cols_f, 32, 16, 2)
     corr[...] = dot_t(rows_f[...], cols_f[...])
 
-    order = (1, 2, 3, 4, 5, 6, 7, 0)
+    order = FAR + (0,)
 
     def ca_copy(i):
-        block = y ^ i
+        block = (y + i) % 8
         return pltpu.make_async_remote_copy(
             src_ref=corr.at[pl.ds(pl.multiple_of((1 - core) * 128 + block * 16, 16), 16)],
             dst_ref=corr_core.at[block],
@@ -446,7 +517,7 @@
         )
 
     def cb_copy(i):
-        block = x ^ i
+        block = (x + i) % 8
         return pltpu.make_async_remote_copy(
             src_ref=proj.at[1 - core, pl.ds(pl.multiple_of(block * 32, 32), 32)],
             dst_ref=proj_core.at[block],
@@ -458,43 +529,43 @@
 
     def ra_copy(i):
         return pltpu.make_async_remote_copy(
-            src_ref=corr_one.at[y ^ i],
+            src_ref=corr_one.at[(y + i) % 8],
             dst_ref=corr_got.at[y],
             send_sem=ra_out.at[i],
             recv_sem=ra_in.at[i],
-            device_id=place(x, y ^ i, z, core),
+            device_id=place(x, (y + i) % 8, z, core),
             device_id_type=MESH,
         )
 
     def rb_copy(i):
         return pltpu.make_async_remote_copy(
-            src_ref=proj_one.at[x ^ i],
+            src_ref=proj_one.at[(x + i) % 8],
             dst_ref=proj_got.at[x],
             send_sem=rb_out.at[i],
             recv_sem=rb_in.at[i],
-            device_id=place(x ^ i, y, z, core),
+            device_id=place((x + i) % 8, y, z, core),
             device_id_type=MESH,
         )
 
     for i in order:
         ca_copy(i).start()
-    for i in range(1, 8):
+    for i in FAR[::-1]:
         g2_copy(i).wait_recv()
-    reorder(last_g, rows_g, cols_g)
+    reorder(last_g, rows_g, cols_g, 4, 2, 32)
     both = dot_t(cols_f[...], rows_g[...]) + dot_t(cols_g[...], rows_f[...])
     proj[0] = both[:, 0:128]
     proj[1] = both[:, 128:256]
     for i in order:
         cb_copy(i).start()
     for i in order:
-        block = y ^ i
+        block = (y + i) % 8
         ca_copy(i).wait_recv()
         rows = pl.ds(pl.multiple_of(core * 128 + block * 16, 16), 16)
         corr_one[block] = corr[rows, :] + corr_core[block]
         if i:
             ra_copy(i).start()
     for i in order:
-        block = x ^ i
+        block = (x + i) % 8
         cb_copy(i).wait_recv()
         rows = pl.ds(pl.multiple_of(block * 32, 32), 32)
         proj_one[block] = proj[core, rows, :] + proj_core[block]
@@ -503,53 +574,60 @@
 
     def sa_copy(i):
         return pltpu.make_async_remote_copy(
-            src_ref=corr_two.at[x ^ i],
+            src_ref=corr_two.at[(x + i) % 8],
             dst_ref=corr_have.at[x],
             send_sem=sa_out.at[i],
             recv_sem=sa_in.at[i],
-            device_id=place(x ^ i, y, z, core),
+            device_id=place((x + i) % 8, y, z, core),
             device_id_type=MESH,
         )
 
     def sb_copy(i):
         return pltpu.make_async_remote_copy(
-            src_ref=proj_two.at[y ^ i],
+            src_ref=proj_two.at[(y + i) % 8],
             dst_ref=proj_have.at[y],
             send_sem=sb_out.at[i],
             recv_sem=sb_in.at[i],
-            device_id=place(x, y ^ i, z, core),
-            device_id_type=MESH,
-        )
-
+            device_id=place(x, (y + i) % 8, z, core),
+            device_id_type=MESH,
+        )
+
+    for i in range(1, 8):
+        g2_copy(i).wait_send()
+    for i in range(1, 16):
+        f2_copy(i).wait_send()
     blank = jnp.zeros((8, 64), jnp.float32)
     total = corr_one[y]
-    for i in range(1, 8):
+    for i in FAR[::-1]:
         ra_copy(i).wait_recv()
-        total += corr_got[y ^ i]
+        total += corr_got[(y + 8 - i) % 8]
     for xx in range(8):
         at = slice(32 * xx, 32 * xx + 32)
         corr_two[xx] = jnp.concatenate([total[0:8, at], total[8:16, at], blank], axis=1)
-    for i in range(1, 8):
+    for i in FAR:
         sa_copy(i).start()
     total = proj_one[x]
-    for i in range(1, 8):
+    for i in FAR[::-1]:
         rb_copy(i).wait_recv()
-        total += proj_got[x ^ i]
+        total += proj_got[(x + 8 - i) % 8]
     for yy in range(8):
         at = slice(16 * yy, 16 * yy + 16)
         proj_two[yy] = jnp.concatenate(
             [total[8 * b : 8 * b + 8, at] for b in range(4)] + [blank], axis=1
         )
-    for i in range(1, 8):
+    for i in FAR:
         sb_copy(i).start()
+    for i in range(8):
+        ca_copy(i).wait_send()
+        cb_copy(i).wait_send()
     one = corr_two[x]
-    for i in range(1, 8):
+    for i in FAR[::-1]:
         sa_copy(i).wait_recv()
-        one += corr_have[x ^ i]
+        one += corr_have[(x + 8 - i) % 8]
     two = proj_two[y]
-    for i in range(1, 8):
+    for i in FAR[::-1]:
         sb_copy(i).wait_recv()
-        two += proj_have[y ^ i]
+        two += proj_have[(y + 8 - i) % 8]
     tile = one + pltpu.roll(two, 64, 1)
 
     sums_z[...] = tile
@@ -560,70 +638,62 @@
             dst_ref=part_z.at[z],
             send_sem=rz_out.at[i],
             recv_sem=rz_in.at[i],
-            device_id=place(x, y, z ^ i, core),
-            device_id_type=MESH,
-        )
-
-    for i in range(1, 8):
+            device_id=place(x, y, (z + i) % 8, core),
+            device_id_type=MESH,
+        )
+
+    for i in FAR:
         rz_copy(i).start()
     for i in range(1, 8):
+        for copy in (ra_copy, rb_copy, sa_copy, sb_copy):
+            copy(i).wait_send()
+    for i in FAR[::-1]:
         rz_copy(i).wait_recv()
-        tile += part_z[z ^ i]
+        tile += part_z[(z + 8 - i) % 8]
     tile = tile * (1.0 / CELLS)
     one = pltpu.roll(tile, (128 - (zh // 2) * 32 - 16 * zl) % 128, 1)
     out_ref[0] = pltpu.roll(one, (zh % 2) * 4, 0)[0:4, 0:16]
     two = pltpu.roll(tile, 64 - 32 * zl - 4 * zh, 1).T
     out_ref[1] = jnp.concatenate([two[0:4, :], two[16:20, :]], axis=1)
 
-    copies[0][0].wait_send()
-    pots[0][0].wait_send()
-    for mine in range(2):
-
-        @pl.when(zl == mine)
-        def _(mine=mine):
-            for copy in outgoing(mine):
-                copy.wait_send()
-
     for i in range(1, 8):
-        for copy in (f_copy, g2_copy, ra_copy, rb_copy, sa_copy, sb_copy, rz_copy):
-            copy(i).wait_send()
-    for i in range(1, 16):
-        g_copy(i).wait_send()
-        f2_copy(i).wait_send()
-    for i in range(8):
-        ca_copy(i).wait_send()
-        cb_copy(i).wait_send()
+        rz_copy(i).wait_send()
 
 
 def on_device(orbitals, potential):
-    halves = orbitals.reshape(8, 2, 2, NY * NZ).transpose(1, 0, 2, 3).reshape(2, 16, NY * NZ)
     f32 = jnp.float32
-    vmem = pl.BlockSpec(memory_space=pltpu.VMEM)
+    hbm = pl.BlockSpec(memory_space=pl.ANY)
     buffers = (
-        [(96, 768), (48, 768), (96, 1024), (72, 1024), (48, 1024), (8, 96, 128)]
-        + [(72, 96), (48, 72), (32, 48), (128, 128), (72, 1024), (576, 128)]
-        + [(8, 32, 128)] * 6
+        [(8, 4, 768), (2, 16, 768), (8, 768)]
+        + [(96, 768), (48, 768), (96, 1024), (72, 1024), (48, 1024), (8, 96, 128)]
+        + [(72, 96), (48, 72), (32, 48), (256, 256), (72, 1024), (288, 256)]
+        + [(8, 32, 128)] * 3
+        + [(16, 16, 128)] * 2
+        + [(8, 32, 128)]
+        + [(16, 16, 128)] * 2
+        + [(8, 32, 128)]
         + [(256, 128)] * 4
         + [(256, 256), (2, 256, 128)]
         + [(8, 16, 256), (8, 32, 128)] * 3
         + [(8, 8, 128)] * 4
         + [(8, 128), (8, 8, 128)]
     )
-    sems = [16, 10, 2] + [8, 8, 16, 16, 16, 16, 8, 8] + [8] * 14
+    sems = [16, 10, 4] + [8, 8, 16, 16, 16, 16, 8, 8] + [8] * 14
     return pl.pallas_call(
         kernel,
         out_shape=jax.ShapeDtypeStruct((2, 4, 16), f32),
-        in_specs=[vmem, vmem],
-        out_specs=vmem,
+        in_specs=[hbm, hbm],
+        out_specs=pl.BlockSpec(memory_space=pltpu.VMEM),
         scratch_shapes=[pltpu.VMEM(shape, f32) for shape in buffers]
-        + [pltpu.SemaphoreType.DMA((count,)) for count in sems],
+        + [pltpu.SemaphoreType.DMA((count,)) for count in sems]
+        + [pltpu.SemaphoreType.REGULAR((3, 2, 4))],
         compiler_params=pltpu.CompilerParams(
-            collective_id=0, has_side_effects=True, vmem_limit_bytes=32 * 1024 * 1024
+            collective_id=0, has_side_effects=True, vmem_limit_bytes=60 * 1024 * 1024
         ),
         cost_estimate=pl.CostEstimate(
             flops=200_000_000, bytes_accessed=1_000_000, transcendentals=0
         ),
-    )(halves, potential)
+    )(orbitals, potential)
 
 
 def solution(mesh):

time: 64.9 us -> 65.4 us (level); the launches traced: 64.6 us -> 64.1 us
  local copies, waits for them, and re-layouts: 2.3 us -> 1.28 us
    reshape x3 -> x0, local copies, waits for them, and re-layouts: 1.05 us -> none  [on_device(): orbitals.reshape(8, 2, 2, NY * NZ).transpose(1, 0, 2, 3)]
where the time goes in v3:
time: 65.4 us; the launch traced here: 64.1 us
  Pallas kernels  62.8 us (96%)
  local copies, waits for them, and re-layouts  1.28 us (2%)
    pallas_call x1, Pallas kernels, on_device(): pl.pallas_call(kernel, out_shape=jax.ShapeDtypeStruct((2, 4, 16), f32), i...  62.8 us

profile of v3, /device:TPU:1, one launch (start us, length us, event | category | flops | bytes accessed | tf_op | source)
XLA Modules:
  0.0 64.1 jit_solution(5708747126551582044)
XLA Ops:
  0.0 62.8 %shard_map.28 = f32[2,4,16]{2,1,0:T(4,128)} custom-call(f32[8,4,768]{2,1,0:T(4,128)} %orb_hbm.1, f32[8,768]{1,0:T(8,128)} %pot_hbm.1), custom_call_target="tpu_custom_call" | custom-call | flops 200000000 | bytes 1000000 | tf_op jit(solution)/shard_map/pallas_call | solution.py:682
  62.8 1.3 %copy.4 = f32[2,4,16]{2,1,0:T(4,128)} copy(f32[2,4,16]{2,1,0:T(4,128)} %shard_map.28) | data formatting | bytes 1024

commit v4 on v2

--- a/solution.py
+++ b/solution.py
@@ -68,7 +68,7 @@
         a,
         b,
         (((1,), (1,)), ((), ())),
-        precision=lax.Precision.HIGHEST,
+        precision=lax.Precision.HIGH,
         preferred_element_type=jnp.float32,
     )
 

time: 64.9 us -> 64.8 us (level)
  no operation moved by 1% of the time
where the time goes in v4:
time: 64.8 us; the launch traced here: 64.5 us
  Pallas kernels  62.2 us (96%)
  local copies, waits for them, and re-layouts  2.3 us (4%)
    pallas_call x1, Pallas kernels, on_device(): pl.pallas_call(kernel, out_shape=jax.ShapeDtypeStruct((2, 4, 16), f32), i...  62.2 us

profile of v4, /device:TPU:1, one launch (start us, length us, event | category | flops | bytes accessed | tf_op | source)
XLA Modules:
  0.0 64.5 jit_solution(4343261307946160622)
XLA Ops:
  0.0 1.0 %reshape.6 = f32[8,2,2,768]{3,2,1,0:T(2,128)S(1)} reshape(f32[8,4,768]{2,1,0:T(4,128)} %param.2) | data formatting | bytes 196608 | tf_op jit(solution)/shard_map/reshape | solution.py:599
  1.0 0.0 copy-start
  1.0 0.1 reshape.7.orb_ref
  1.1 0.7 %copy-done = f32[8,768]{1,0:T(8,128)S(1)} copy-done((f32[8,768]{1,0:T(8,128)S(1)}, f32[8,768]{1,0:T(8,128)}, u32[]{:S(2)}) %copy-start) | copy-done | bytes 24600
  1.7 62.2 %shard_map.28 = f32[2,4,16]{2,1,0:T(4,128)S(1)} custom-call(f32[2,16,768]{2,1,0:T(8,128)S(1)} %reshape.7.orb_ref, f32[8,768]{1,0:T(8,128)S(1)} %copy-done), custom_call_target="tpu_custom_call" | custom-call | flops 200000000 | bytes 1000000 | tf_op jit(solution)/shard_map/pallas_call | solution.py:613
  63.9 0.6 copy.7
  (1 shorter events, 0.0 us)
Async XLA Ops:
  1.0 0.7 %copy-start = (f32[8,768]{1,0:T(8,128)S(1)}, f32[8,768]{1,0:T(8,128)}, u32[]{:S(2)}) copy-start(f32[8,768]{1,0:T(8,128)} %pot_ref.1) | copy-start | bytes 73732
